TPU v7x, 32 devices: a whole 2x2x4 slice. The times are simulated.
32 devices in a mesh: half: 2 (over x), dp: 8 (over z, core), mp: 2 (over y).
Axes of the slice: x: 2, y: 2, z: 4, core: 2. Of those that a mesh axis runs over, the one named last changes fastest.
Arguments:
- samples: bfloat16 [4, 16, 1024, 512], P(None, ('half', 'dp')), may hold values from -6 to 6
- seg_ids: int32 [4, 16, 1024], P(None, ('half', 'dp')), may hold values from 0 to 3, never falling along the last dimension, each value on 1 to 512 neighbouring positions
- data_ids: int32 [4, 16, 4], P(None, ('half', 'dp')), may hold values from 0 to 7, as said below
- test_rows: bfloat16 [4, 8192, 100], P(None, ('half', 'dp', 'mp')), may hold values from -6 to 6
- test_data: int32 [4, 8192], P(None, ('half', 'dp', 'mp')), may hold values from 0 to 7
- labels: int32 [4, 8192], P(None, ('half', 'dp', 'mp')), may hold values from 0 to 9
- norm_params: bfloat16 [4, 512], P(None, ('half', 'dp')), may hold values from -1.75 to 1.75
- w_qkv: bfloat16 [512, 3, 512], P(('half', 'dp'), None, 'mp'), may hold values from -0.25 to 0.25
- w_out: bfloat16 [512, 512], P('mp', ('half', 'dp')), may hold values from -2 to 2
- w_up: bfloat16 [512, 1024], P(('half', 'dp'), 'mp'), may hold values from -0.25 to 0.25
- w_down: bfloat16 [1024, 512], P('mp', ('half', 'dp')), may hold values from -0.1875 to 0.1875
- pool_value: bfloat16 [512, 512], P(('half', 'dp')), may hold values from -0.25 to 0.25
- pool_query: bfloat16 [4, 512], P(None, ('half', 'dp')), may hold values from -0.5 to 0.5
- w_dec: bfloat16 [512, 4032], replicated, may hold values from -0.15625 to 0.15625
- child_in: bfloat16 [32, 512], replicated, may hold values from -1 to 1
- child_out: bfloat16 [32, 512], replicated, may hold values from -0.25 to 0.25
Outputs:
- total_loss: float32 [], replicated
- grad_samples: float32 [4, 16, 1024, 512], P(None, ('half', 'dp'), 'mp')
- grad_norm_params: float32 [4, 512], P(None, ('half', 'dp'))
- grad_w_qkv: float32 [512, 3, 512], P(('half', 'dp'), None, 'mp')
- grad_w_out: float32 [512, 512], P('mp', ('half', 'dp'))
- grad_w_up: float32 [512, 1024], P(('half', 'dp'), 'mp')
- grad_w_down: float32 [1024, 512], P('mp', ('half', 'dp'))
- grad_pool_value: float32 [512, 512], P(('half', 'dp'))
- grad_pool_query: float32 [4, 512], P(None, ('half', 'dp'))
- grad_w_dec: float32 [512, 4032], replicated
- grad_child_in: float32 [32, 512], replicated
- grad_child_out: float32 [32, 512], replicated
Inputs may be any that keep to these rules, and one draw needn't show every extreme that they name: `data_ids`: in every micro-batch, each dataset number of each half names some segment of that half's sequences, and the first segment of every sequence of one half has one dataset number.
All inputs are finite; a program needn't handle non-finite values.
Results may differ from a plain program's by a relative error of at most 0.029.
Values may be sent and summed in bfloat16 or wider, within the bound.
No kernel may reach another device: no remote copies, remote signals or barrier semaphores. Data moves between devices by JAX's collectives and lax.ppermute only.
A program may use at most 256 MiB of HBM per device.

v0:
```python
import math

import jax
import jax.numpy as jnp
from jax import lax
from jax.sharding import PartitionSpec as P

NH = 4
HD = 128
F = 100
H = 512
C = 10
R = 32
NSEG = 4
NDS = 8


EPSILON = 1e-05
NEG_FILL = -1e30
HIGHEST = lax.Precision.HIGHEST


def combined_all(value, axis, join):
    pieces = jax.tree.map(lambda part: lax.all_gather(part, axis), value)
    head = jax.tree.map(lambda part: part[0], pieces)
    tail = jax.tree.map(lambda part: part[1:], pieces)
    subtotal, _ = lax.scan(lambda subtotal, section: (join(subtotal, section), None), head, tail)
    return subtotal


def from_partner(value, axis, distance):
    return lax.ppermute(value, axis, [(i, i ^ 1 << distance) for i in range(lax.axis_size(axis))])


def layer_norm(values, gain_row, shift_row):
    center = values - jnp.mean(values, -1, keepdims=True)
    spread = jnp.mean(center * center, -1, keepdims=True)
    return center * lax.rsqrt(spread + EPSILON) * (1.0 + gain_row) + shift_row


def exact_gelu(values):
    return jax.nn.gelu(values, approximate=False)


def row_term(source, weight, pattern):
    return jnp.einsum(pattern, source, weight, preferred_element_type=jnp.float32)


def combine_pools(earlier, later):
    peak_both = jnp.maximum(earlier[0], later[0])
    scale_one = jnp.exp(earlier[0] - peak_both)
    scale_two = jnp.exp(later[0] - peak_both)
    return (
        peak_both,
        earlier[1] * scale_one + later[1] * scale_two,
        earlier[2] * scale_one[..., None] + later[2] * scale_two[..., None],
    )


def attend_forward(query_seq, key_seq, value_seq, seg_seq, block_rows):
    length, local_heads, head_size = query_seq.shape
    scale_root = math.sqrt(head_size)
    block_count = length // block_rows
    query_blocks = query_seq.reshape(block_count, block_rows, local_heads, head_size)
    seg_blocks = seg_seq.reshape(block_count, block_rows)

    def one_block(block_pair):
        query_blk, seg_blk = block_pair
        scores = (
            jnp.einsum("qhe,khe->hqk", query_blk, key_seq, preferred_element_type=jnp.float32)
            / scale_root
        )
        same_seg = (seg_blk[:, None] == seg_seq[None, :])[None]
        scores = jnp.where(same_seg, scores, NEG_FILL)
        row_peak = jnp.max(scores, -1, keepdims=True)
        exponent = jnp.exp(scores - row_peak)
        row_total = jnp.sum(exponent, -1, keepdims=True)
        weights = (exponent / row_total).astype(jnp.bfloat16)
        attended_output = jnp.einsum(
            "hqk,khe->qhe", weights, value_seq, preferred_element_type=jnp.float32
        )
        return (attended_output.astype(jnp.bfloat16), (row_peak + jnp.log(row_total))[:, :, 0])

    attended_output, log_sums = lax.map(one_block, (query_blocks, seg_blocks))
    return (attended_output.reshape(length, local_heads * head_size), log_sums)


def attend_backward(query_seq, key_seq, value_seq, seg_seq, grad_seq, log_sums, block_rows):
    length, local_heads, head_size = query_seq.shape
    scale_root = math.sqrt(head_size)
    block_count = length // block_rows
    query_blocks = query_seq.reshape(block_count, block_rows, local_heads, head_size)
    grad_blocks = grad_seq.reshape(block_count, block_rows, local_heads, head_size)
    seg_blocks = seg_seq.reshape(block_count, block_rows)

    def one_block(carried, block_set):
        key_grad, value_grad = carried
        query_blk, grad_blk, seg_blk, lse_blk = block_set
        scores = (
            jnp.einsum("qhe,khe->hqk", query_blk, key_seq, preferred_element_type=jnp.float32)
            / scale_root
        )
        same_seg = (seg_blk[:, None] == seg_seq[None, :])[None]
        weights = jnp.where(same_seg, jnp.exp(scores - lse_blk[:, :, None]), 0.0)
        grad_weights = jnp.einsum(
            "qhe,khe->hqk", grad_blk, value_seq, preferred_element_type=jnp.float32
        )
        inner_sum = jnp.sum(weights * grad_weights, -1, keepdims=True)
        grad_scores = (weights * (grad_weights - inner_sum)).astype(jnp.bfloat16)
        query_grad = (
            jnp.einsum("hqk,khe->qhe", grad_scores, key_seq, preferred_element_type=jnp.float32)
            / scale_root
        )
        key_grad = (
            key_grad
            + jnp.einsum("hqk,qhe->khe", grad_scores, query_blk, preferred_element_type=jnp.float32)
            / scale_root
        )
        value_grad = value_grad + jnp.einsum(
            "hqk,qhe->khe",
            weights.astype(jnp.bfloat16),
            grad_blk,
            preferred_element_type=jnp.float32,
        )
        return ((key_grad, value_grad), query_grad)

    zero_grad = jnp.zeros((length, local_heads, head_size), jnp.float32)
    (key_grad, value_grad), query_grad = lax.scan(
        one_block, (zero_grad, zero_grad), (query_blocks, grad_blocks, seg_blocks, log_sums)
    )
    width = local_heads * head_size
    return jnp.stack(
        [
            query_grad.reshape(length, width),
            key_grad.reshape(length, width),
            value_grad.reshape(length, width),
        ],
        1,
    )


def child_pass(row_inputs, row_data, row_labels, coef_low, in_weight, out_weight, row_total):
    row_count = row_inputs.shape[0]
    selector = (row_data[:, None] == jnp.arange(NDS, dtype=jnp.int32)[None, :]).astype(jnp.float32)
    first_cols = coef_low[:, : F * R].reshape(NDS, F, R).transpose(1, 0, 2).reshape(F, NDS * R)
    second_cols = coef_low[:, F * R : (F + C) * R].astype(jnp.float32)
    offsets = coef_low[:, (F + C) * R :].astype(jnp.float32)
    projected = jnp.dot(row_inputs, first_cols, preferred_element_type=jnp.float32).reshape(
        row_count, NDS, R
    )
    reduced = jnp.sum(selector[:, :, None] * projected, 1)
    reduced_low = reduced.astype(jnp.bfloat16)
    before = jnp.dot(reduced_low, in_weight, preferred_element_type=jnp.float32) + jnp.dot(
        selector, offsets, precision=HIGHEST
    )
    hidden_vals, gelu_back = jax.vjp(exact_gelu, before)
    hidden_low = hidden_vals.astype(jnp.bfloat16)
    narrow = jnp.einsum("rh,kh->rk", hidden_low, out_weight, preferred_element_type=jnp.float32)
    picked = jnp.dot(selector, second_cols, precision=HIGHEST).reshape(row_count, C, R)
    logits = jnp.sum(narrow[:, None, :] * picked, -1)
    row_peak = jnp.max(logits, -1, keepdims=True)
    shifted = jnp.exp(logits - row_peak)
    row_sums = jnp.sum(shifted, -1, keepdims=True)
    target = (row_labels[:, None] == jnp.arange(C, dtype=jnp.int32)[None, :]).astype(jnp.float32)
    losses = row_peak[:, 0] + jnp.log(row_sums[:, 0]) - jnp.sum(logits * target, -1)
    loss_part = jnp.sum(losses) / row_total
    logit_grad = (shifted / row_sums - target) / row_total
    narrow_grad = jnp.sum(logit_grad[:, :, None] * picked, 1)
    picked_grad = (logit_grad[:, :, None] * narrow[:, None, :]).reshape(row_count, C * R)
    second_grad = jnp.dot(selector.T, picked_grad, precision=HIGHEST)
    hidden_grad = jnp.dot(narrow_grad, out_weight.astype(jnp.float32), precision=HIGHEST)
    out_part = jnp.dot(narrow_grad.T, hidden_low.astype(jnp.float32), precision=HIGHEST)
    (before_grad,) = gelu_back(hidden_grad)
    offset_grad = jnp.dot(selector.T, before_grad, precision=HIGHEST)
    reduced_grad = jnp.dot(before_grad, in_weight.astype(jnp.float32).T, precision=HIGHEST)
    in_part = jnp.dot(reduced_low.astype(jnp.float32).T, before_grad, precision=HIGHEST)
    spread_grad = (selector[:, :, None] * reduced_grad[:, None, :]).reshape(row_count, NDS * R)
    first_grad = jnp.dot(row_inputs.astype(jnp.float32).T, spread_grad, precision=HIGHEST)
    first_grad = first_grad.reshape(F, NDS, R).transpose(1, 0, 2).reshape(NDS, F * R)
    coef_grad = jnp.concatenate([first_grad, second_grad, offset_grad], 1)
    return (coef_grad, in_part, out_part, loss_part)


def local(
    samples,
    seg_ids,
    data_ids,
    test_rows,
    test_data,
    labels,
    norm_params,
    w_qkv,
    w_out,
    w_up,
    w_down,
    pool_value,
    pool_query,
    w_dec,
    child_in,
    child_out,
):
    micro_count = samples.shape[0]
    seq_count = samples.shape[1]
    length = samples.shape[2]
    model_width = samples.shape[3]
    mp_size = lax.axis_size("mp")
    mp_index = lax.axis_index("mp")
    half_len = length // mp_size
    head_size = HD
    local_heads = w_qkv.shape[2] // head_size
    block_rows = min(512, length)
    row_total = (
        micro_count * test_rows.shape[1] * lax.axis_size("half") * lax.axis_size("dp") * mp_size
    )
    qkv_acc = jnp.zeros((model_width, 3, w_qkv.shape[2]), jnp.float32)
    outw_acc = jnp.zeros((w_out.shape[0], model_width), jnp.float32)
    up_acc = jnp.zeros((model_width, w_up.shape[1]), jnp.float32)
    down_acc = jnp.zeros((w_down.shape[0], model_width), jnp.float32)
    norm_acc = jnp.zeros((4, model_width), jnp.float32)
    pvalue_acc = jnp.zeros((model_width, model_width), jnp.float32)
    pquery_acc = jnp.zeros((NH, model_width), jnp.float32)
    dec_acc = jnp.zeros(w_dec.shape, jnp.float32)
    child_in_acc = jnp.zeros((R, H), jnp.float32)
    child_out_acc = jnp.zeros((R, H), jnp.float32)
    loss_acc = jnp.zeros((), jnp.float32)
    sample_grads = []
    for batch_idx in range(micro_count):
        fetched = (
            lax.all_gather(w_qkv, ("half", "dp"), axis=0, tiled=True),
            lax.all_gather(w_out, ("half", "dp"), axis=1, tiled=True),
            lax.all_gather(w_up, ("half", "dp"), axis=0, tiled=True),
            lax.all_gather(w_down, ("half", "dp"), axis=1, tiled=True),
            lax.all_gather(norm_params, ("half", "dp"), axis=1, tiled=True),
            lax.all_gather(pool_value, ("half", "dp"), axis=0, tiled=True),
            lax.all_gather(pool_query, ("half", "dp"), axis=1, tiled=True),
        )
        full_weights = fetched + (None, None)
        (
            query_key_value_weight,
            output_matrix,
            up_matrix,
            down_matrix,
            norms_full,
            pvalue_w,
            pquery_w,
            qkv_wide,
            out_wide,
        ) = full_weights
        norms_float = norms_full.astype(jnp.float32)
        token_rows = samples[batch_idx]
        segments = seg_ids[batch_idx]
        projected = jnp.einsum(
            "zwt,tky->zwky", token_rows, query_key_value_weight, preferred_element_type=jnp.float32
        ).astype(jnp.bfloat16)
        split_heads = projected.reshape(seq_count, length, 3, local_heads, head_size)

        def forward_seq(seq_set):
            one_seq, seg_seq = seq_set
            return attend_forward(one_seq[:, 0], one_seq[:, 1], one_seq[:, 2], seg_seq, block_rows)

        attended_output, log_sums = lax.map(forward_seq, (split_heads, segments))
        attn_half = lax.psum_scatter(
            row_term(attended_output, output_matrix, "scn,nd->csd"),
            "mp",
            scatter_dimension=0,
            tiled=True,
        ).transpose(1, 0, 2)
        own_tokens = lax.dynamic_slice_in_dim(token_rows, mp_index * half_len, half_len, 1).astype(
            jnp.float32
        )
        first_in = own_tokens + attn_half
        first_norm, first_back = jax.vjp(layer_norm, first_in, norms_float[0], norms_float[1])
        first_low = first_norm.astype(jnp.bfloat16)
        first_complete = lax.all_gather(first_low, "mp", axis=1, tiled=True)
        upward_projected = jnp.einsum(
            "rzm,mi->rzi", first_complete, up_matrix, preferred_element_type=jnp.float32
        )
        active_vals, gelu_back = jax.vjp(exact_gelu, upward_projected)
        active_mask_rows = active_vals.astype(jnp.bfloat16)
        ffn_half = (
            lax.psum_scatter(
                row_term(active_mask_rows, down_matrix, "scf,fd->csd").astype(jnp.bfloat16),
                "mp",
                scatter_dimension=0,
                tiled=True,
            )
            .astype(jnp.float32)
            .transpose(1, 0, 2)
        )
        second_in = first_norm + ffn_half
        encoded, second_back = jax.vjp(layer_norm, second_in, norms_float[2], norms_float[3])
        enc_low = encoded.astype(jnp.bfloat16).reshape(-1, model_width)
        own_segs = lax.dynamic_slice_in_dim(segments, mp_index * half_len, half_len, 1)
        seq_data = data_ids[batch_idx]
        token_data = jnp.zeros_like(own_segs)
        for segment in range(NSEG):
            token_data = jnp.where(
                own_segs == segment, seq_data[:, segment : segment + 1], token_data
            )
        member = token_data.reshape(-1)[:, None] == jnp.arange(NDS, dtype=jnp.int32)[None, :]
        pool_scores = jnp.einsum("nd,hd->nh", enc_low, pquery_w, preferred_element_type=jnp.float32)
        pool_vals = jnp.dot(enc_low, pvalue_w, preferred_element_type=jnp.float32).reshape(
            -1, NH, head_size
        )
        masked = jnp.where(member[:, :, None], pool_scores[:, None, :], NEG_FILL)
        local_peak = jnp.max(masked, 0)
        local_weight = jnp.where(member[:, :, None], jnp.exp(masked - local_peak[None]), 0.0)
        local_total = jnp.sum(local_weight, 0)
        local_acc = jnp.einsum("ndh,nhe->dhe", local_weight, pool_vals, precision=HIGHEST)
        peak_all, total_all, accum = combined_all(
            (local_peak, local_total, local_acc), ("dp", "mp"), combine_pools
        )
        pooled = accum / total_all[..., None]
        pooled_low = pooled.reshape(NDS, model_width).astype(jnp.bfloat16)
        coef_low = jnp.dot(pooled_low, w_dec, preferred_element_type=jnp.float32).astype(
            jnp.bfloat16
        )
        other_coef, other_pooled = from_partner((coef_low, pooled_low), "half", 0)
        coef_part, in_part, out_part, loss_part = child_pass(
            test_rows[batch_idx],
            test_data[batch_idx],
            labels[batch_idx],
            other_coef,
            child_in,
            child_out,
            row_total,
        )
        summed = lax.psum((coef_part, in_part, out_part, loss_part), ("dp", "mp"))
        returned = (
            from_partner(summed[0].astype(jnp.bfloat16), "half", 0).astype(jnp.float32),
            from_partner(summed[1].astype(jnp.bfloat16), "half", 0).astype(jnp.float32),
            from_partner(summed[2].astype(jnp.bfloat16), "half", 0).astype(jnp.float32),
            from_partner(summed[3].astype(jnp.bfloat16), "half", 0).astype(jnp.float32),
        )
        grad_coef = returned[0].astype(jnp.bfloat16)
        other_grad = summed[0].astype(jnp.bfloat16)
        own_term = jnp.einsum(
            "dk,de->ke", pooled_low, grad_coef, preferred_element_type=jnp.float32
        )
        other_term = jnp.einsum(
            "dk,de->ke", other_pooled, other_grad, preferred_element_type=jnp.float32
        )
        dec_acc = dec_acc + (own_term + other_term)
        child_in_acc = child_in_acc + (summed[1] + returned[1])
        child_out_acc = child_out_acc + (summed[2] + returned[2])
        loss_acc = loss_acc + (summed[3] + returned[3])
        pooled_grad = jnp.einsum(
            "de,ke->dk", grad_coef, w_dec, preferred_element_type=jnp.float32
        ).reshape(NDS, NH, head_size)
        weights = local_weight * jnp.exp(local_peak - peak_all)[None] / total_all[None]
        val_grad = (
            jnp.einsum("ndh,dhe->nhe", weights, pooled_grad, precision=HIGHEST)
            .reshape(-1, model_width)
            .astype(jnp.bfloat16)
        )
        weight_grad = jnp.einsum("dhe,nhe->ndh", pooled_grad, pool_vals, precision=HIGHEST)
        centre = jnp.sum(pooled_grad * pooled, -1)
        score_grad = jnp.sum(weights * (weight_grad - centre[None]), 1).astype(jnp.bfloat16)
        pvalue_acc = pvalue_acc + jnp.einsum(
            "nd,ne->de", enc_low, val_grad, preferred_element_type=jnp.float32
        )
        pquery_acc = pquery_acc + jnp.einsum(
            "nh,nd->hd", score_grad, enc_low, preferred_element_type=jnp.float32
        )
        enc_grad = jnp.einsum("ne,de->nd", val_grad, pvalue_w, preferred_element_type=jnp.float32)
        enc_grad = enc_grad + jnp.einsum(
            "nh,hd->nd", score_grad, pquery_w, preferred_element_type=jnp.float32
        )
        enc_grad = enc_grad.reshape(seq_count, half_len, model_width)
        second_grad, gain_two, shift_two = second_back(enc_grad)
        ffn_grad = second_grad.astype(jnp.bfloat16)
        feedforward_complete = lax.all_gather(ffn_grad, "mp", axis=1, tiled=True)
        down_acc = down_acc + jnp.einsum(
            "mgx,mgn->xn",
            active_mask_rows,
            feedforward_complete,
            preferred_element_type=jnp.float32,
        )
        activation_gradient = jnp.einsum(
            "yjt,mt->yjm", feedforward_complete, down_matrix, preferred_element_type=jnp.float32
        )
        (rise_grad,) = gelu_back(activation_gradient)
        rising_lowrank = rise_grad.astype(jnp.bfloat16)
        up_acc = up_acc + jnp.einsum(
            "maw,mag->wg", first_complete, rising_lowrank, preferred_element_type=jnp.float32
        )
        first_back_half = (
            lax.psum_scatter(
                row_term(rising_lowrank, up_matrix, "scf,df->csd").astype(jnp.bfloat16),
                "mp",
                scatter_dimension=0,
                tiled=True,
            )
            .astype(jnp.float32)
            .transpose(1, 0, 2)
        )
        first_in_grad, gain_one, shift_one = first_back(second_grad + first_back_half)
        attn_grad = first_in_grad.astype(jnp.bfloat16)
        attention_complete = lax.all_gather(attn_grad, "mp", axis=1, tiled=True)
        outw_acc = outw_acc + jnp.einsum(
            "fzh,fzc->hc", attended_output, attention_complete, preferred_element_type=jnp.float32
        )
        heads_grad = jnp.einsum(
            "hba,oa->hbo", attention_complete, output_matrix, preferred_element_type=jnp.float32
        ).astype(jnp.bfloat16)

        def backward_seq(seq_set):
            one_seq, seg_seq, grad_seq, lse_seq = seq_set
            return attend_backward(
                one_seq[:, 0],
                one_seq[:, 1],
                one_seq[:, 2],
                seg_seq,
                grad_seq.reshape(length, local_heads, head_size),
                lse_seq,
                block_rows,
            )

        query_key_value_gradient = lax.map(
            backward_seq, (split_heads, segments, heads_grad, log_sums)
        ).astype(jnp.bfloat16)
        qkv_acc = qkv_acc + jnp.einsum(
            "koj,kozh->jzh",
            token_rows,
            query_key_value_gradient,
            preferred_element_type=jnp.float32,
        )
        token_back = (
            lax.psum_scatter(
                row_term(query_key_value_gradient, query_key_value_weight, "scgn,dgn->csd").astype(
                    jnp.bfloat16
                ),
                "mp",
                scatter_dimension=0,
                tiled=True,
            )
            .astype(jnp.float32)
            .transpose(1, 0, 2)
        )
        sample_grads.append(first_in_grad + token_back)
        norm_acc = norm_acc + jnp.stack([gain_one, shift_one, gain_two, shift_two])
    owned = (
        lax.psum_scatter(qkv_acc, ("half", "dp"), scatter_dimension=0, tiled=True),
        lax.psum_scatter(outw_acc, ("half", "dp"), scatter_dimension=1, tiled=True),
        lax.psum_scatter(up_acc, ("half", "dp"), scatter_dimension=0, tiled=True),
        lax.psum_scatter(down_acc, ("half", "dp"), scatter_dimension=1, tiled=True),
        lax.psum_scatter(norm_acc, ("half", "dp"), scatter_dimension=1, tiled=True),
        lax.psum_scatter(pvalue_acc, ("half", "dp"), scatter_dimension=0, tiled=True),
        lax.psum_scatter(pquery_acc, ("half", "dp"), scatter_dimension=1, tiled=True),
    )
    outw_share = owned[1]
    norm_share, value_share, query_share = lax.psum((owned[4], owned[5], owned[6]), "mp")
    return (
        loss_acc,
        jnp.stack(sample_grads),
        norm_share,
        owned[0],
        outw_share,
        owned[2],
        owned[3],
        value_share,
        query_share,
        dec_acc,
        child_in_acc,
        child_out_acc,
    )


def solution(mesh):
    placed = (
        P(None, ("half", "dp"), None, None),
        P(None, ("half", "dp"), None),
        P(None, ("half", "dp"), None),
        P(None, ("half", "dp", "mp"), None),
        P(None, ("half", "dp", "mp")),
        P(None, ("half", "dp", "mp")),
        P(None, ("half", "dp")),
        P(("half", "dp"), None, "mp"),
        P("mp", ("half", "dp")),
        P(("half", "dp"), "mp"),
        P("mp", ("half", "dp")),
        P(("half", "dp"), None),
        P(None, ("half", "dp")),
        P(),
        P(),
        P(),
    )
    return jax.shard_map(
        local,
        mesh=mesh,
        in_specs=placed,
        out_specs=(
            P(),
            P(None, ("half", "dp"), "mp", None),
            P(None, ("half", "dp")),
            P(("half", "dp"), None, "mp"),
            P("mp", ("half", "dp")),
            P(("half", "dp"), "mp"),
            P("mp", ("half", "dp")),
            P(("half", "dp"), None),
            P(None, ("half", "dp")),
            P(),
            P(),
            P(),
        ),
        check_vma=False,
    )
```

profile of v0, /device:TPU:0, one launch (start us, length us, event | category | flops | bytes accessed | tf_op | source)
XLA Modules:
  0.0 2081.2 jit_solution(6547223099507756055)
XLA Ops:
  178.1 31.3 %reduce-scatter.39.cloned.1.call-done = f32[512,1,512]{2,0,1:T(8,128)} async-done(((f32[1024,1,512]{2,0,1:T(8,128)}), f32[512,1,512]{2,0,1:T(8,128)}) %reduce-scatter.39.cloned.1.call-update) | async-done | bytes 1048592 | tf_op jit(solution)/shard_map/reduce_scatter | solution.py:262
  402.8 31.3 %all-gather.22 = f32[16,8,4]{1,2,0:T(4,128)S(1)} all-gather(f32[1,8,4]{1,2,0:T(4,128)S(1)} %bitcast.1598), channel_id=2, replica_groups=mesh['half'=2,'dp'=8,'mp'=2] {'dp','mp'}, dimensions={0}, use_global_device_ids=true | all-gather | bytes 2176 | tf_op jit(solution)/shard_map/all_gather | solution.py:24
  435.3 28.6 %all-gather.23 = f32[16,8,4]{1,2,0:T(4,128)S(1)} all-gather(f32[1,8,4]{1,2,0:T(4,128)S(1)} %bitcast.1661), channel_id=3, replica_groups=mesh['half'=2,'dp'=8,'mp'=2] {'dp','mp'}, dimensions={0}, use_global_device_ids=true | all-gather | bytes 2176 | tf_op jit(solution)/shard_map/all_gather | solution.py:24
  468.1 32.3 %all-gather.2 = f32[128,4,128]{2,0,1:T(8,128)S(1)} all-gather(f32[8,4,128]{2,0,1:T(8,128)S(1)} %convolution_bitcast_fusion.19), channel_id=4, replica_groups=mesh['half'=2,'dp'=8,'mp'=2] {'dp','mp'}, dimensions={0}, use_global_device_ids=true | all-gather | bytes 278528 | tf_op jit(solution)/shard_map/all_gather | solution.py:24
  504.4 28.6 %all-gather.24 = f32[16,8,4]{1,2,0:T(4,128)S(1)} all-gather(f32[1,8,4]{1,2,0:T(4,128)S(1)} %bitcast.1599), channel_id=5, replica_groups=mesh['half'=2,'dp'=8,'mp'=2] {'dp','mp'}, dimensions={0}, use_global_device_ids=true | all-gather | bytes 2176 | tf_op jit(solution)/shard_map/all_gather | solution.py:24
  533.6 31.2 %all-gather.25 = f32[16,8,4]{1,2,0:T(4,128)S(1)} all-gather(f32[1,8,4]{1,2,0:T(4,128)S(1)} %bitcast.1662), channel_id=6, replica_groups=mesh['half'=2,'dp'=8,'mp'=2] {'dp','mp'}, dimensions={0}, use_global_device_ids=true | all-gather | bytes 2176 | tf_op jit(solution)/shard_map/all_gather | solution.py:24
  568.1 29.8 %all-gather.5 = f32[128,4,128]{2,0,1:T(8,128)S(1)} all-gather(f32[8,4,128]{2,0,1:T(8,128)S(1)} %convolution_bitcast_fusion.18), channel_id=7, replica_groups=mesh['half'=2,'dp'=8,'mp'=2] {'dp','mp'}, dimensions={0}, use_global_device_ids=true | all-gather | bytes 278528 | tf_op jit(solution)/shard_map/all_gather | solution.py:24
  599.2 30.8 %all-gather.26 = f32[16,8,4]{1,2,0:T(4,128)S(1)} all-gather(f32[1,8,4]{1,2,0:T(4,128)S(1)} %bitcast.1600), channel_id=8, replica_groups=mesh['half'=2,'dp'=8,'mp'=2] {'dp','mp'}, dimensions={0}, use_global_device_ids=true | all-gather | bytes 2176 | tf_op jit(solution)/shard_map/all_gather | solution.py:24
  630.7 28.6 %all-gather.27 = f32[16,8,4]{1,2,0:T(4,128)S(1)} all-gather(f32[1,8,4]{1,2,0:T(4,128)S(1)} %bitcast.1663), channel_id=9, replica_groups=mesh['half'=2,'dp'=8,'mp'=2] {'dp','mp'}, dimensions={0}, use_global_device_ids=true | all-gather | bytes 2176 | tf_op jit(solution)/shard_map/all_gather | solution.py:24
  660.4 32.3 %all-gather.8 = f32[128,4,128]{2,0,1:T(8,128)S(1)} all-gather(f32[8,4,128]{2,0,1:T(8,128)S(1)} %convolution_bitcast_fusion.17), channel_id=10, replica_groups=mesh['half'=2,'dp'=8,'mp'=2] {'dp','mp'}, dimensions={0}, use_global_device_ids=true | all-gather | bytes 278528 | tf_op jit(solution)/shard_map/all_gather | solution.py:24
  695.4 28.7 %all-gather.28 = f32[16,8,4]{1,2,0:T(4,128)S(1)} all-gather(f32[1,8,4]{1,2,0:T(4,128)S(1)} %bitcast.1601), channel_id=11, replica_groups=mesh['half'=2,'dp'=8,'mp'=2] {'dp','mp'}, dimensions={0}, use_global_device_ids=true | all-gather | bytes 2176 | tf_op jit(solution)/shard_map/all_gather | solution.py:24
  724.7 30.8 %all-gather.29 = f32[16,8,4]{1,2,0:T(4,128)S(1)} all-gather(f32[1,8,4]{1,2,0:T(4,128)S(1)} %bitcast.1664), channel_id=12, replica_groups=mesh['half'=2,'dp'=8,'mp'=2] {'dp','mp'}, dimensions={0}, use_global_device_ids=true | all-gather | bytes 2176 | tf_op jit(solution)/shard_map/all_gather | solution.py:24
  757.5 29.8 %all-gather.11 = f32[128,4,128]{2,0,1:T(8,128)S(1)} all-gather(f32[8,4,128]{2,0,1:T(8,128)S(1)} %convolution_bitcast_fusion.16), channel_id=13, replica_groups=mesh['half'=2,'dp'=8,'mp'=2] {'dp','mp'}, dimensions={0}, use_global_device_ids=true | all-gather | bytes 278528 | tf_op jit(solution)/shard_map/all_gather | solution.py:24
  788.1 25.5 %while.237 = (s32[]{:T(128)}, f32[8,4]{0,1:T(4,128)S(1)}, f32[8,4]{0,1:T(4,128)S(1)}, f32[8,4,128]{2,1,0:T(4,128)S(1)}, f32[15,8,4]{1,2,0:T(4,128)}, /*index=5*/...) while((s32[]{:T(128)}, f32[8,4]{0,1:T(4,128)S(1)}, f32[8,4]{0,1:T(4,128)S(1)}, ...), condition=%wide.region_13.14_spmd, body=%wide.region_12.13_spmd.sunk | while | flops 12482 | bytes 83813 | solution.py:27
  1013.0 67.2 %all-reduce.14 = (f32[]{:T(128)}, f32[]{:T(128)}, f32[]{:T(128)}, f32[]{:T(128)}, bf16[8,4032]{1,0:T(8,128)(2,1)}, /*index=5*/bf16[8,4032]{1,0:T(8,128)(2,1)}, bf16[8,4032]{1,0:T(8,128)(2,1)}, bf16[8,4032]{1,0:T(8,128)(2,1)}) all-reduce(f32[]{:T(128)S(6)} %div.390, ...), channel_id=1, replica_groups=mesh['half'=2,'dp'=8,'mp'=2] {'dp','mp'}, use_global_device_ids=true, to_apply=%region_20.21 | all-reduce | flops 129028 | bytes 774176 | tf_op jit(solution)/shard_map/psum | solution.py:328
  1337.9 30.0 %while.247 = (s32[]{:T(128)}, f32[1024,2,128]{0,2,1:T(8,128)}, f32[1024,2,128]{0,2,1:T(8,128)}, bf16[2,512,2,128]{3,1,2,0:T(8,128)(2,1)}, bf16[2,512,2,128]{3,1,...) while((s32[]{:T(128)}, f32[1024,2,128]{0,2,1:T(8,128)}, ...), condition=%wide.region_134.135_spmd.clone, body=%wide.region_132.134_spmd.clone.sunk | while | flops 1359870976 | bytes 79206680 | solution.py:128
  1376.5 30.4 %while.246 = (s32[]{:T(128)}, f32[1024,2,128]{0,2,1:T(8,128)}, f32[1024,2,128]{0,2,1:T(8,128)}, bf16[2,512,2,128]{3,1,2,0:T(8,128)(2,1)}, bf16[2,512,2,128]{3,1,...) while((s32[]{:T(128)}, f32[1024,2,128]{0,2,1:T(8,128)}, ...), condition=%wide.region_121.122_spmd.clone, body=%wide.region_119.121_spmd.clone.sunk | while | flops 1359870976 | bytes 79206680 | solution.py:128
  1415.7 30.3 %while.245 = (s32[]{:T(128)}, f32[1024,2,128]{0,2,1:T(8,128)}, f32[1024,2,128]{0,2,1:T(8,128)}, bf16[2,512,2,128]{3,1,2,0:T(8,128)(2,1)}, bf16[2,512,2,128]{3,1,...) while((s32[]{:T(128)}, f32[1024,2,128]{0,2,1:T(8,128)}, ...), condition=%wide.region_108.109_spmd.clone, body=%wide.region_106.108_spmd.clone.sunk | while | flops 1359870976 | bytes 79206680 | solution.py:128
  1454.7 30.3 %while.244 = (s32[]{:T(128)}, f32[1024,2,128]{0,2,1:T(8,128)}, f32[1024,2,128]{0,2,1:T(8,128)}, bf16[2,512,2,128]{3,1,2,0:T(8,128)(2,1)}, bf16[2,512,2,128]{3,1,...) while((s32[]{:T(128)}, f32[1024,2,128]{0,2,1:T(8,128)}, ...), condition=%wide.region_95.96_spmd.clone, body=%wide.region_93.95_spmd.clone.sunk | while | flops 1359870976 | bytes 79206680 | solution.py:128
  1647.3 28.9 %reduce-scatter.67.cloned.1.call-done = f32[32,4]{1,0:T(8,128)} async-done(((f32[512,4]{1,0:T(8,128)}), f32[32,4]{1,0:T(8,128)}) %reduce-scatter.67.cloned.1.call-update) | async-done | bytes 528
  1686.0 91.6 %all-reduce.11.cloned.1.call-done = f32[512,3,256]{2,1,0:T(4,128)} async-done(((f32[512,3,256]{2,1,0:T(4,128)}), f32[512,3,256]{2,1,0:T(4,128)}) %all-reduce.11.cloned.1.call-update) | async-done | bytes 1572880
  1890.1 61.7 %reduce-scatter.61.cloned.1.call-done = f32[32,512]{1,0:T(8,128)} async-done(((f32[512,512]{1,0:T(8,128)}), f32[32,512]{1,0:T(8,128)}) %reduce-scatter.61.cloned.1.call-update) | async-done | bytes 65552 | tf_op jit(solution)/shard_map/reduce_scatter | solution.py:445
  1951.8 60.9 %reduce-scatter.63.cloned.1.call-done = f32[512,32]{0,1:T(8,128)} async-done(((f32[512,512]{0,1:T(8,128)}), f32[512,32]{0,1:T(8,128)}) %reduce-scatter.63.cloned.1.call-update) | async-done | bytes 65552 | tf_op jit(solution)/shard_map/reduce_scatter | solution.py:446
  2012.7 58.8 %reduce-scatter.59.cloned.1.call-done = f32[256,32]{0,1:T(8,128)} async-done(((f32[256,512]{0,1:T(8,128)}), f32[256,32]{0,1:T(8,128)}) %reduce-scatter.59.cloned.1.call-update) | async-done | bytes 32784 | tf_op jit(solution)/shard_map/reduce_scatter | solution.py:444
  (1969 shorter events, 1392.6 us)
Async XLA Ops:
  7.2 161.5 %reduce-scatter.27.cloned.1.call-start = ((), (), s32[]{:S(2)}) async-start(), calls=%async_computation.22 | async-start | bytes 3145728 | tf_op jit(solution)/shard_map/reduce_scatter | solution.py:262
  146.0 114.9 %all-gather.47.cloned.1.call-start = ((), (), s32[]{:S(2)}) async-start(), calls=%async_computation.29 | async-start | bytes 1572864 | tf_op jit(solution)/shard_map/all_gather | solution.py:274
  214.5 112.0 %all-gather.43.cloned.1.call-start = ((), (), s32[]{:S(2)}) async-start(), calls=%async_computation.23 | async-start | bytes 1572864 | tf_op jit(solution)/shard_map/all_gather | solution.py:274
  336.8 813.4 %all-gather.59.cloned.1.call-start = ((), (), s32[]{:S(2)}) async-start(), calls=%async_computation.51 | async-start | bytes 1572864 | tf_op jit(solution)/shard_map/all_gather | solution.py:372
  817.8 129.7 %collective-permute-start = (bf16[8,4032]{1,0:T(8,128)(2,1)}, bf16[8,4032]{1,0:T(8,128)(2,1)}, u32[]{:S(2)}, u32[]{:S(2)}) collective-permute-start(bf16[8,4032]{1,0:T(8,128)(2,1)} %convolution_convert_fusion.3), channel_id=1, source_target_pairs={{0,16},{16,0},{1,17},{17,1},{2,18},{18,2},{3,19},{19,3},{4,20},{20... | collective-permute-start | bytes 193544 | tf_op jit(solution)/shard_map/ppermute | solution.py:32
  1138.8 102.0 %reduce-scatter.51.cloned.1.call-start = ((), (), s32[]{:S(2)}) async-start(), calls=%async_computation.38 | async-start | bytes 1572864 | tf_op jit(solution)/shard_map/reduce_scatter | solution.py:388
  1157.0 107.0 %reduce-scatter.55.cloned.1.call-start = ((), (), s32[]{:S(2)}) async-start(), calls=%async_computation.40 | async-start | bytes 1572864 | tf_op jit(solution)/shard_map/reduce_scatter | solution.py:388
  1179.7 107.5 %reduce-scatter.43.cloned.1.call-start = ((), (), s32[]{:S(2)}) async-start(), calls=%async_computation.34 | async-start | bytes 1572864 | tf_op jit(solution)/shard_map/reduce_scatter | solution.py:388
  1202.4 107.3 %reduce-scatter.47.cloned.1.call-start = ((), (), s32[]{:S(2)}) async-start(), calls=%async_computation.36 | async-start | bytes 1572864 | tf_op jit(solution)/shard_map/reduce_scatter | solution.py:388
  1225.2 109.1 %all-gather.65.cloned.1.call-start = ((), (), s32[]{:S(2)}) async-start(), calls=%async_computation.54 | async-start | bytes 1572864 | tf_op jit(solution)/shard_map/all_gather | solution.py:399
  1319.7 131.5 %all-gather.53.cloned.1.call-start = ((), (), s32[]{:S(2)}) async-start(), calls=%async_computation.48 | async-start | bytes 1572864 | tf_op jit(solution)/shard_map/all_gather | solution.py:399
  1323.6 246.8 %reduce-scatter.65.cloned.1.call-start = ((), (), s32[]{:S(2)}) async-start(), calls=%async_computation.45 | async-start | bytes 1114112 | tf_op jit(solution)/shard_map/reduce_scatter | solution.py:448
  1327.6 268.8 %reduce-scatter.69.cloned.1.call-start = ((), (), s32[]{:S(2)}) async-start(), calls=%async_computation.56 | async-start | bytes 278528
  1332.1 284.5 %all-reduce.13.cloned.1.call-start = ((), (), s32[]{:S(2)}) async-start(), calls=%async_computation.58 | async-start | bytes 1048576 | tf_op jit(solution)/shard_map/psum | solution.py:328
  1333.1 343.1 %reduce-scatter.67.cloned.1.call-start = ((), (), s32[]{:S(2)}) async-start(), calls=%async_computation.55 | async-start | bytes 278528
  1334.3 443.3 %all-reduce.11.cloned.1.call-start = ((), (), s32[]{:S(2)}) async-start(), calls=%async_computation.57 | async-start | bytes 4194304
  1498.8 300.4 %reduce-scatter.57.cloned.1.call-start = ((), (), s32[]{:S(2)}) async-start(), calls=%async_computation.41 | async-start | bytes 1572864 | tf_op jit(solution)/shard_map/reduce_scatter | solution.py:429
  1501.9 320.1 %reduce-scatter.53.cloned.1.call-start = ((), (), s32[]{:S(2)}) async-start(), calls=%async_computation.39 | async-start | bytes 1572864 | tf_op jit(solution)/shard_map/reduce_scatter | solution.py:429
  1505.5 339.0 %reduce-scatter.49.cloned.1.call-start = ((), (), s32[]{:S(2)}) async-start(), calls=%async_computation.37 | async-start | bytes 1572864 | tf_op jit(solution)/shard_map/reduce_scatter | solution.py:429
  1507.6 359.5 %reduce-scatter.45.cloned.1.call-start = ((), (), s32[]{:S(2)}) async-start(), calls=%async_computation.35 | async-start | bytes 1572864 | tf_op jit(solution)/shard_map/reduce_scatter | solution.py:429
  1553.0 337.1 %all-reduce.9.cloned.1.call-start = ((), (), s32[]{:S(2)}) async-start(), calls=%async_computation.46 | async-start | bytes 131072 | tf_op jit(solution)/shard_map/psum | solution.py:452
  1570.4 381.4 %reduce-scatter.61.cloned.1.call-start = ((), (), s32[]{:S(2)}) async-start(), calls=%async_computation.43 | async-start | bytes 1114112 | tf_op jit(solution)/shard_map/reduce_scatter | solution.py:445
  1573.0 439.7 %reduce-scatter.63.cloned.1.call-start = ((), (), s32[]{:S(2)}) async-start(), calls=%async_computation.44 | async-start | bytes 1114112 | tf_op jit(solution)/shard_map/reduce_scatter | solution.py:446
  1640.4 431.2 %reduce-scatter.59.cloned.1.call-start = ((), (), s32[]{:S(2)}) async-start(), calls=%async_computation.42 | async-start | bytes 557056 | tf_op jit(solution)/shard_map/reduce_scatter | solution.py:444
  (499 other events, 14269.2 us)
Sparse Core Ops, SparseCore 0:
  76.0 30.3 reduce-scatter.26
  109.3 31.8 reduce-scatter.30
  143.4 31.8 reduce-scatter.34
  177.5 31.8 reduce-scatter.38
  213.3 21.3 all-gather.46
  236.6 21.2 all-gather.44
  259.5 21.2 all-gather.48
  282.4 21.2 all-gather.42
  1151.6 21.2 all-gather.62
  1174.3 21.2 all-gather.50
  1197.0 21.2 all-gather.54
  1311.8 21.2 all-gather.64
  1334.7 21.2 all-gather.60
  1357.6 21.2 all-gather.56
  1380.3 21.2 all-gather.52
  1405.3 57.4 reduce-scatter.64
  1466.6 54.2 reduce-scatter.68
  1525.6 90.9 all-reduce.12
  1620.6 55.6 reduce-scatter.66
  1680.8 96.7 all-reduce.10
  1869.3 20.7 all-reduce.8
  1894.3 57.4 reduce-scatter.60
  1956.3 56.3 reduce-scatter.62
  2016.7 54.8 reduce-scatter.58
  (13 shorter events, 260.4 us)
where the time goes:
time: 2100 us; the launch traced here: 2080 us
  waiting for transfers between devices  630 us (30%)
  blocking collectives  586 us (28%)
  matrix products  412 us (20%)
  local copies, waits for them, and re-layouts  200 us (10%)
  other arithmetic  185 us (9%)
  starting transfers between devices  33.8 us (2%)
  between operations  31.9 us (2%)
    all_gather x12, blocking collectives, combined_all(): pieces = jax.tree.map(lambda part: lax.all_gather(part, axis), value)  363 us
    unnamed x40, waiting for transfers between devices  122 us
    reduce_scatter x4, waiting for transfers between devices, local(): lax.psum_scatter(row_term(query_key_value_gradient, query_key_value_weigh...  81.3 us
    reduce_scatter x4, waiting for transfers between devices, local(): lax.psum_scatter(row_term(rising_lowrank, up_matrix, 'scf,df->csd').astyp...  75.1 us
    psum x1, blocking collectives, local(): summed = lax.psum((coef_part, in_part, out_part, loss_part), ('dp', 'mp'))  67.2 us
    reduce_scatter x1, waiting for transfers between devices, local(): lax.psum_scatter(up_acc, ('half', 'dp'), scatter_dimension=0, tiled=True)  61.7 us
    reduce_scatter x1, waiting for transfers between devices, local(): lax.psum_scatter(down_acc, ('half', 'dp'), scatter_dimension=1, tiled=True)  60.9 us
    all_gather x4, waiting for transfers between devices, local(): feedforward_complete = lax.all_gather(ffn_grad, 'mp', axis=1, tiled=True)  59 us
  transfers between devices with their start and end apart: 61, of which 27 were waited for; matrix products, arithmetic and copies ran while one was open for 29% of the time, Pallas kernels for 0%

commit v1 on v0

v1 whole, which is shorter than its diff:
```python
import math

import jax
import jax.numpy as jnp
from jax import lax
from jax.sharding import PartitionSpec as P

NH = 4
HD = 128
F = 100
H = 512
C = 10
R = 32
NSEG = 4
NDS = 8


EPSILON = 1e-05
NEG_FILL = -1e30
HIGHEST = lax.Precision.HIGHEST
BF = jnp.bfloat16
F32 = jnp.float32


def dot(a, b, dims):
    return lax.dot_general(a, b, (dims, ((), ())), preferred_element_type=F32)


def swap(value, axis, bit):
    size = lax.axis_size(axis)
    return lax.ppermute(value, axis, [(i, i ^ (1 << bit)) for i in range(size)])


def bit_of(axis, bit):
    return lax.rem(lax.div(lax.axis_index(axis), 1 << bit), 2)


def ordered(mine, theirs, bit):
    low = jnp.where(bit == 0, mine, theirs)
    high = jnp.where(bit == 0, theirs, mine)
    return low, high


def hd_stages():
    count = lax.axis_size("dp").bit_length() - 1
    return [("dp", b) for b in range(count - 1, 0, -1)], ("half", 0), ("dp", 0)


def significance(stage):
    return 1000 if stage[0] == "half" else stage[1]


def gather_rows(value, stages):
    rows, cols = value.shape
    done = []
    for stage in stages:
        place = sum(significance(d) > significance(stage) for d in done)
        theirs = swap(value, *stage)
        value = jnp.stack(ordered(value, theirs, bit_of(*stage)), place)
        done.append(stage)
    return value.reshape(-1, cols)


def scatter_rows(value, stages, count):
    cols = value.shape[-1]
    left = sorted(stages, key=significance, reverse=True)
    value = value.reshape((2,) * len(left) + (value.shape[0] // count, cols))
    for stage in stages:
        place = left.index(stage)
        bit = bit_of(*stage)
        first = lax.index_in_dim(value, 0, place, False)
        second = lax.index_in_dim(value, 1, place, False)
        keep = jnp.where(bit == 0, first, second)
        give = jnp.where(bit == 0, second, first).astype(BF)
        value = keep + swap(give, *stage).astype(F32)
        left.remove(stage)
    return value


def sum_over(value, stages):
    for stage in stages:
        low, high = ordered(value, swap(value, *stage), bit_of(*stage))
        value = low + high
    return value


def combine_pools(earlier, later):
    peak_both = jnp.maximum(earlier[0], later[0])
    scale_one = jnp.exp(earlier[0] - peak_both)
    scale_two = jnp.exp(later[0] - peak_both)
    return (
        peak_both,
        earlier[1] * scale_one + later[1] * scale_two,
        earlier[2] * scale_one[..., None] + later[2] * scale_two[..., None],
    )


def normalise(values):
    center = values - jnp.mean(values, -1, keepdims=True)
    inverse = lax.rsqrt(jnp.mean(center * center, -1, keepdims=True) + EPSILON)
    return center * inverse, inverse


def normalise_back(grad, gain, scaled, inverse):
    inner = grad * (1.0 + gain)
    mean_one = jnp.mean(inner, -1, keepdims=True)
    mean_two = jnp.mean(inner * scaled, -1, keepdims=True)
    return inverse * (inner - mean_one - scaled * mean_two)


def gelu_both(values):
    cdf = 0.5 * (1.0 + lax.erf(values * math.sqrt(0.5)))
    density = jnp.exp(-0.5 * values * values) * (1.0 / math.sqrt(2.0 * math.pi))
    return values * cdf, cdf + values * density


def attend_forward(qkv, seg):
    batch, length = seg.shape
    heads = qkv.shape[-1] // (3 * HD)
    parts = qkv.reshape(batch, length, 3, heads, HD)

    def one(pair):
        part, row_seg = pair
        scores = jnp.einsum("qhe,khe->hqk", part[:, 0], part[:, 1], preferred_element_type=F32)
        scores = scores * (1.0 / math.sqrt(HD))
        scores = jnp.where((row_seg[:, None] == row_seg[None, :])[None], scores, NEG_FILL)
        peak = jnp.max(scores, -1, keepdims=True)
        shifted = jnp.exp(scores - peak)
        total = jnp.sum(shifted, -1, keepdims=True)
        out = jnp.einsum(
            "hqk,khe->qhe", (shifted / total).astype(BF), part[:, 2], preferred_element_type=F32
        )
        return out.astype(BF).reshape(length, heads * HD), (peak + jnp.log(total))[:, :, 0]

    outs, sums = lax.map(one, (parts, seg))
    return outs.reshape(batch * length, heads * HD), sums


def attend_backward(qkv, seg, grad, sums):
    batch, length = seg.shape
    heads = qkv.shape[-1] // (3 * HD)
    parts = qkv.reshape(batch, length, 3, heads, HD)
    grads = grad.reshape(batch, length, heads, HD)
    root = 1.0 / math.sqrt(HD)

    def one(group):
        part, row_seg, out_grad, log_sum = group
        query, key, value = part[:, 0], part[:, 1], part[:, 2]
        scores = jnp.einsum("qhe,khe->hqk", query, key, preferred_element_type=F32) * root
        same = (row_seg[:, None] == row_seg[None, :])[None]
        probs = jnp.where(same, jnp.exp(scores - log_sum[:, :, None]), 0.0)
        prob_grad = jnp.einsum("qhe,khe->hqk", out_grad, value, preferred_element_type=F32)
        inner = jnp.sum(probs * prob_grad, -1, keepdims=True)
        score_grad = (probs * (prob_grad - inner)).astype(BF)
        dq = jnp.einsum("hqk,khe->qhe", score_grad, key, preferred_element_type=F32) * root
        dk = jnp.einsum("hqk,qhe->khe", score_grad, query, preferred_element_type=F32) * root
        dv = jnp.einsum("hqk,qhe->khe", probs.astype(BF), out_grad, preferred_element_type=F32)
        return jnp.stack([dq, dk, dv], 1).astype(BF).reshape(length, 3 * heads * HD)

    return lax.map(one, (parts, seg, grads, sums)).reshape(batch * length, 3 * heads * HD)


def child_pass(row_inputs, row_data, row_labels, coef_low, in_weight, out_weight, row_total):
    row_count = row_inputs.shape[0]
    selector = (row_data[:, None] == jnp.arange(NDS, dtype=jnp.int32)[None, :]).astype(F32)
    first_cols = coef_low[:, : F * R].reshape(NDS, F, R).transpose(1, 0, 2).reshape(F, NDS * R)
    second_cols = coef_low[:, F * R : (F + C) * R].astype(F32)
    offsets = coef_low[:, (F + C) * R :].astype(F32)
    projected = jnp.dot(row_inputs, first_cols, preferred_element_type=F32)
    projected = projected.reshape(row_count, NDS, R)
    reduced_low = jnp.sum(selector[:, :, None] * projected, 1).astype(BF)
    before = jnp.dot(reduced_low, in_weight, preferred_element_type=F32) + jnp.dot(
        selector, offsets, precision=HIGHEST
    )
    hidden, slope = gelu_both(before)
    hidden_low = hidden.astype(BF)
    narrow = jnp.einsum("rh,kh->rk", hidden_low, out_weight, preferred_element_type=F32)
    picked = jnp.dot(selector, second_cols, precision=HIGHEST).reshape(row_count, C, R)
    logits = jnp.sum(narrow[:, None, :] * picked, -1)
    row_peak = jnp.max(logits, -1, keepdims=True)
    shifted = jnp.exp(logits - row_peak)
    row_sums = jnp.sum(shifted, -1, keepdims=True)
    target = (row_labels[:, None] == jnp.arange(C, dtype=jnp.int32)[None, :]).astype(F32)
    losses = row_peak[:, 0] + jnp.log(row_sums[:, 0]) - jnp.sum(logits * target, -1)
    loss_part = jnp.sum(losses) / row_total
    logit_grad = (shifted / row_sums - target) / row_total
    narrow_grad = jnp.sum(logit_grad[:, :, None] * picked, 1)
    picked_grad = (logit_grad[:, :, None] * narrow[:, None, :]).reshape(row_count, C * R)
    second_grad = jnp.dot(selector.T, picked_grad, precision=HIGHEST)
    hidden_grad = jnp.dot(narrow_grad, out_weight.astype(F32), precision=HIGHEST)
    out_part = jnp.dot(narrow_grad.T, hidden_low.astype(F32), precision=HIGHEST)
    before_grad = hidden_grad * slope
    offset_grad = jnp.dot(selector.T, before_grad, precision=HIGHEST)
    reduced_grad = jnp.dot(before_grad, in_weight.astype(F32).T, precision=HIGHEST)
    in_part = jnp.dot(reduced_low.astype(F32).T, before_grad, precision=HIGHEST)
    spread_grad = (selector[:, :, None] * reduced_grad[:, None, :]).reshape(row_count, NDS * R)
    first_grad = jnp.dot(row_inputs.astype(F32).T, spread_grad, precision=HIGHEST)
    first_grad = first_grad.reshape(F, NDS, R).transpose(1, 0, 2).reshape(NDS, F * R)
    coef_grad = jnp.concatenate([first_grad, second_grad, offset_grad], 1)
    return coef_grad, in_part, out_part, loss_part


def local(
    samples,
    seg_ids,
    data_ids,
    test_rows,
    test_data,
    labels,
    norm_params,
    w_qkv,
    w_out,
    w_up,
    w_down,
    pool_value,
    pool_query,
    w_dec,
    child_in,
    child_out,
):
    micro, seqs, length, width = samples.shape
    mp_size = lax.axis_size("mp")
    mp_index = lax.axis_index("mp")
    half_index = lax.axis_index("half")
    own = micro // mp_size
    shards = lax.axis_size("half") * lax.axis_size("dp")
    depth = w_qkv.shape[0]
    cols = w_qkv.shape[2]
    units = w_up.shape[1]
    row_total = micro * test_rows.shape[1] * shards * mp_size
    far, half_stage, core_stage = hd_stages()
    mp_stage = ("mp", 0)

    qkv_mine = gather_rows(w_qkv.reshape(depth, 3 * cols), far + [half_stage, core_stage])
    qkv_other = swap(qkv_mine, *mp_stage)
    extra = jnp.pad(jnp.concatenate([pool_query.T, norm_params.T], 1), ((0, 0), (0, 120)))
    shared = jnp.concatenate([w_out.T, w_up, w_down.T], 1)
    packed = jnp.concatenate([shared, swap(shared, *mp_stage), pool_value, extra], 1)
    packed = gather_rows(packed, [half_stage] + far + [core_stage])
    wide = cols + 2 * units

    def both(start, count):
        return jnp.concatenate(
            [packed[:, start : start + count], packed[:, wide + start : wide + start + count]], 1
        )

    out_t = both(0, cols)
    up_w = both(cols, units)
    down_t = both(cols + units, units)
    pvalue_w = packed[:, 2 * wide : 2 * wide + width]
    tail = packed[:, 2 * wide + width :].T
    pquery_w = tail[:NH]
    norms = tail[NH : NH + 4].astype(F32)

    start = mp_index * own
    tokens = lax.dynamic_slice_in_dim(samples, start, own, 0).reshape(own * seqs * length, width)
    seg = lax.dynamic_slice_in_dim(seg_ids, start, own, 0).reshape(own * seqs, length)
    seq_data = lax.dynamic_slice_in_dim(data_ids, start, own, 0).reshape(own * seqs, NSEG)
    qkv_a = dot(tokens, qkv_mine, ((1,), (0,))).astype(BF)
    heads_a, sums_a = attend_forward(qkv_a, seg)
    qkv_b = dot(tokens, qkv_other, ((1,), (0,))).astype(BF)
    heads_b, sums_b = attend_forward(qkv_b, seg)
    heads = jnp.concatenate([heads_a, heads_b], 1)
    attn = dot(heads, out_t, ((1,), (1,)))
    one_scaled, one_inverse = normalise(tokens.astype(F32) + attn)
    first = one_scaled * (1.0 + norms[0]) + norms[1]
    first_low = first.astype(BF)
    up = dot(first_low, up_w, ((1,), (0,)))
    act, slope = gelu_both(up)
    act = act.astype(BF)
    two_scaled, two_inverse = normalise(first + dot(act, down_t, ((1,), (1,))))
    enc_low = (two_scaled * (1.0 + norms[2]) + norms[3]).astype(BF)
    pool_val = dot(enc_low, pvalue_w, ((1,), (0,)))
    pool_score = dot(enc_low, pquery_w, ((1,), (1,)))

    token_data = jnp.zeros_like(seg)
    for segment in range(NSEG):
        token_data = jnp.where(seg == segment, seq_data[:, segment : segment + 1], token_data)
    member = token_data.reshape(own, seqs * length, 1) == jnp.arange(NDS, dtype=jnp.int32)
    member = member[..., None]
    scores = pool_score.reshape(own, seqs * length, 1, NH)
    vals = pool_val.reshape(own, seqs * length, NH, HD)
    masked = jnp.where(member, scores, NEG_FILL)
    peak = jnp.max(masked, 1)
    weight = jnp.where(member, jnp.exp(masked - peak[:, None]), 0.0)
    pools = (peak, jnp.sum(weight, 1), jnp.einsum("mndh,mnhe->mdhe", weight, vals))
    for stage in [core_stage] + far:
        theirs = jax.tree.map(lambda part: swap(part, *stage), pools)
        bit = bit_of(*stage)
        pairs = [ordered(a, b, bit) for a, b in zip(pools, theirs)]
        pools = combine_pools([p[0] for p in pairs], [p[1] for p in pairs])
    peak, total, accum = pools
    pooled = (accum / total[..., None]).reshape(own * NDS, width)
    pooled_low = pooled.astype(BF)

    def across(value, flip):
        pairs = [(i, i ^ flip) for i in range(2 * mp_size)]
        return lax.ppermute(value, ("half", "mp"), pairs)

    other_pooled = jnp.concatenate(
        ordered(across(pooled_low, mp_size), across(pooled_low, mp_size + 1), mp_index)
    )
    own_pooled = jnp.concatenate(ordered(pooled_low, across(pooled_low, 1), mp_index))
    coef = dot(other_pooled, w_dec, ((1,), (0,))).astype(BF).reshape(micro, NDS, -1)
    coef_grads, in_parts, out_parts, loss_parts = [], 0.0, 0.0, 0.0
    for m in range(micro):
        coef_part, in_part, out_part, loss_part = child_pass(
            test_rows[m], test_data[m], labels[m], coef[m], child_in, child_out, row_total
        )
        coef_grads.append(coef_part)
        in_parts = in_parts + in_part
        out_parts = out_parts + out_part
        loss_parts = loss_parts + loss_part
    coef_grad = jnp.concatenate(coef_grads, 0)

    part = dot(coef_grad.astype(BF), w_dec, ((1,), (1,)))
    low_part, high_part = part[: own * NDS], part[own * NDS :]
    same_mp = jnp.where(mp_index == 0, low_part, high_part)
    other_mp = jnp.where(mp_index == 0, high_part, low_part)
    pooled_grad = across(same_mp, mp_size) + across(other_mp, mp_size + 1)
    pooled_grad = sum_over(pooled_grad, [core_stage] + far)

    summed = lax.psum(
        jnp.concatenate([coef_grad.reshape(-1), in_parts.reshape(-1), out_parts.reshape(-1)]),
        ("dp", "mp"),
    )
    loss_sum = lax.psum(loss_parts, ("dp", "mp"))
    coef_size = coef_grad.size
    summed_coef = summed[:coef_size].reshape(coef_grad.shape).astype(BF)
    summed_child = summed[coef_size:].reshape(2, R, H)
    theirs_coef = swap(summed_coef, "half", 0)
    coef_all = jnp.concatenate(ordered(theirs_coef, summed_coef, half_index))
    pooled_all = jnp.concatenate(ordered(own_pooled, other_pooled, half_index))
    dec_grad = dot(pooled_all, coef_all, ((0,), (0,)))
    child_grad = summed_child + swap(summed_child, "half", 0)
    loss = loss_sum + swap(loss_sum, "half", 0)

    pooled_grad = pooled_grad.reshape(own, NDS, NH, HD)
    pool_w = jnp.where(member, jnp.exp(scores - peak[:, None]), 0.0) / total[:, None]
    val_grad = jnp.einsum("mndh,mdhe->mnhe", pool_w, pooled_grad).reshape(-1, width).astype(BF)
    weight_grad = jnp.einsum("mdhe,mnhe->mndh", pooled_grad, vals)
    centre = jnp.sum(pooled_grad * pooled.reshape(pooled_grad.shape), -1)
    score_grad = jnp.sum(pool_w * (weight_grad - centre[:, None]), 2).reshape(-1, NH).astype(BF)
    g_pvalue = dot(enc_low, val_grad, ((0,), (0,)))
    g_pquery = dot(enc_low, score_grad, ((0,), (0,)))
    enc_grad = dot(val_grad, pvalue_w, ((1,), (1,))) + dot(score_grad, pquery_w, ((1,), (0,)))
    g_gain_two = jnp.sum(enc_grad * two_scaled, 0)
    g_shift_two = jnp.sum(enc_grad, 0)
    second_grad = normalise_back(enc_grad, norms[2], two_scaled, two_inverse)
    ffn_grad = second_grad.astype(BF)
    g_down = dot(ffn_grad, act, ((0,), (0,)))
    up_grad = (dot(ffn_grad, down_t, ((1,), (0,))) * slope).astype(BF)
    g_up = dot(first_low, up_grad, ((0,), (0,)))
    first_grad = second_grad + dot(up_grad, up_w, ((1,), (1,)))
    g_gain_one = jnp.sum(first_grad * one_scaled, 0)
    g_shift_one = jnp.sum(first_grad, 0)
    input_grad = normalise_back(first_grad, norms[0], one_scaled, one_inverse)
    attn_grad = input_grad.astype(BF)
    g_out = dot(attn_grad, heads, ((0,), (0,)))
    heads_grad = dot(attn_grad, out_t, ((1,), (0,))).astype(BF)

    back_a = attend_backward(qkv_a, seg, heads_grad[:, :cols], sums_a)
    back_b = attend_backward(qkv_b, seg, heads_grad[:, cols:], sums_b)
    g_qkv_a = dot(tokens, back_a, ((0,), (0,)))
    g_qkv_b = dot(tokens, back_b, ((0,), (0,)))
    token_grad = (
        input_grad + dot(back_a, qkv_mine, ((1,), (1,))) + dot(back_b, qkv_other, ((1,), (1,)))
    )

    def give_mp(mine, other):
        return mine + swap(other.astype(BF), *mp_stage).astype(F32)

    order = [core_stage, half_stage] + far[::-1]
    early_mine = jnp.concatenate([g_out[:, :cols], g_up[:, :units], g_down[:, :units]], 1)
    early_other = jnp.concatenate([g_out[:, cols:], g_up[:, units:], g_down[:, units:]], 1)
    early = scatter_rows(give_mp(early_mine, early_other), order, shards)
    late = scatter_rows(give_mp(g_qkv_a, g_qkv_b), order, shards)
    norm_rows = jnp.stack([g_gain_one, g_shift_one, g_gain_two, g_shift_two], 1)
    small = jnp.concatenate([g_pvalue, g_pquery, norm_rows], 1)
    small = jnp.pad(small, ((0, 0), (0, 120)))
    small = scatter_rows(small, order, shards)
    small = small + swap(small, *mp_stage)

    token_grad = token_grad.reshape(own, seqs, mp_size, length // mp_size, width)
    keep = lax.dynamic_index_in_dim(token_grad, mp_index, 2, False)
    give = lax.dynamic_index_in_dim(token_grad, 1 - mp_index, 2, False).astype(BF)
    sample_grad = jnp.concatenate(ordered(keep, swap(give, *mp_stage).astype(F32), mp_index), 0)

    return (
        loss,
        sample_grad,
        small[:, width + NH : width + NH + 4].T,
        late.reshape(depth, 3, cols),
        early[:, :cols].T,
        early[:, cols : cols + units],
        early[:, cols + units :].T,
        small[:, :width],
        small[:, width : width + NH].T,
        dec_grad,
        child_grad[0],
        child_grad[1],
    )


def solution(mesh):
    placed = (
        P(None, ("half", "dp"), None, None),
        P(None, ("half", "dp"), None),
        P(None, ("half", "dp"), None),
        P(None, ("half", "dp", "mp"), None),
        P(None, ("half", "dp", "mp")),
        P(None, ("half", "dp", "mp")),
        P(None, ("half", "dp")),
        P(("half", "dp"), None, "mp"),
        P("mp", ("half", "dp")),
        P(("half", "dp"), "mp"),
        P("mp", ("half", "dp")),
        P(("half", "dp"), None),
        P(None, ("half", "dp")),
        P(),
        P(),
        P(),
    )
    return jax.shard_map(
        local,
        mesh=mesh,
        in_specs=placed,
        out_specs=(
            P(),
            P(None, ("half", "dp"), "mp", None),
            P(None, ("half", "dp")),
            P(("half", "dp"), None, "mp"),
            P("mp", ("half", "dp")),
            P(("half", "dp"), "mp"),
            P("mp", ("half", "dp")),
            P(("half", "dp"), None),
            P(None, ("half", "dp")),
            P(),
            P(),
            P(),
        ),
        check_vma=False,
    )
```

time: 2100 us -> 637 us (0.30)
  blocking collectives: 586 us -> 31.5 us
  waiting for transfers between devices: 630 us -> 90.3 us
  matrix products: 412 us -> 190 us
  other arithmetic: 185 us -> 85.8 us
  local copies, waits for them, and re-layouts: 200 us -> 167 us
    all_gather x19 -> x0, blocking collectives: 514 us -> none  [the longest x12 363 us: combined_all(): pieces = jax.tree.map(lambda part: lax.all_gather(part, axis), value)]
    reduce_scatter x20 -> x0, waiting for transfers between devices: 405 us -> none  [the longest x4 81.3 us: local(): lax.psum_scatter(row_term(query_key_value_gradient, query_key_value_weigh...]
    dot_general x188 -> x87, matrix products: 388 us -> 167 us  [the longest x24 77.8 us: dot(): return lax.dot_general(a, b, (dims, ((), ())), preferred_element_type=F32)]
    unnamed x40 -> x1, waiting for transfers between devices: 122 us -> 0.02 us
    ppermute x24 -> x46, waiting for transfers between devices: 4.93 us -> 90.3 us  [the longest x41 87.9 us: swap(): return lax.ppermute(value, axis, [(i, i ^ 1 << bit) for i in range(size)])]
    all_gather x12 -> x0, waiting for transfers between devices: 59.1 us -> none  [the longest x4 59 us: local(): feedforward_complete = lax.all_gather(ffn_grad, 'mp', axis=1, tiled=True)]
    dynamic_slice x84 -> x15, local copies, waits for them, and re-layouts: 54.2 us -> 8.81 us  [the longest x4 5.64 us: attend_backward(): lax.map(one, (parts, seg, grads, sums))]
    psum x2 -> x1, blocking collectives: 72.7 us -> 31.5 us  [local(): loss_sum = lax.psum(loss_parts, ('dp', 'mp'))]
  transfers between devices with their start and end apart: 61 -> 47, of which waited for: 27 -> 21; matrix products, arithmetic and copies ran while one was open for 29% -> 65% of each run, Pallas kernels for 0% -> 0%
where the time goes in v1:
time: 637 us; the launch traced here: 628 us
  matrix products  190 us (30%)
  local copies, waits for them, and re-layouts  167 us (26%)
  waiting for transfers between devices  90.3 us (14%)
  other arithmetic  85.8 us (13%)
  starting transfers between devices  40.3 us (6%)
  blocking collectives  31.5 us (5%)
  between operations  21.8 us (3%)
    ppermute x41, waiting for transfers between devices, swap(): return lax.ppermute(value, axis, [(i, i ^ 1 << bit) for i in range(size)])  87.9 us
    dot_general x24, matrix products, dot(): return lax.dot_general(a, b, (dims, ((), ())), preferred_element_type=F32)  77.8 us
    ppermute x41, starting transfers between devices, swap(): return lax.ppermute(value, axis, [(i, i ^ 1 << bit) for i in range(size)])  34.7 us
    psum x1, blocking collectives, local(): loss_sum = lax.psum(loss_parts, ('dp', 'mp'))  31.5 us
    unnamed x293, local copies, waits for them, and re-layouts  22.3 us
    reshape x2, local copies, waits for them, and re-layouts, attend_forward(): parts = qkv.reshape(batch, length, 3, heads, HD)  14 us
  transfers between devices with their start and end apart: 47, of which 21 were waited for; matrix products, arithmetic and copies ran while one was open for 65% of the time, Pallas kernels for 0%

profile of v1, /device:TPU:0, one launch (start us, length us, event | category | flops | bytes accessed | tf_op | source)
XLA Modules:
  0.0 628.2 jit_solution(13272942821023948323)
XLA Ops:
  31.7 4.2 collective-permute-done.6
  39.1 14.9 %collective-permute-done.7 = bf16[2,32,3200]{2,1,0:T(8,128)(2,1)S(1)} collective-permute-done((bf16[2,32,3200]{2,1,0:T(8,128)(2,1)}, bf16[2,32,3200]{2,1,0:T(8,128)(2,1)S(1)}, u32[]{:S(2)}, u32[]{:S(2)}) %collective-permute-start.7) | collective-permute-done | bytes 409632 | tf_op jit(solution)/shard_map/ppermute | solution.py:31
  57.5 4.6 convolution_convert_fusion.2
  62.1 7.1 %reshape.1034 = bf16[2,1024,3,2,128]{4,3,2,1,0:T(2,128)(2,1)} reshape(bf16[2048,768]{1,0:T(8,128)(2,1)} %convolution_convert_fusion.2) | data formatting | bytes 6291456 | tf_op jit(solution)/shard_map/reshape | solution.py:120
  74.3 20.2 %while.44 = (s32[]{:T(128)}, bf16[2,1024,256]{2,1,0:T(8,128)(2,1)}, f32[2,2,1024]{2,1,0:T(2,128)S(1)}, bf16[2,1024,3,2,128]{4,1,3,2,0:T(8,128)(2,1)}, s32[2,1024]{1,0:T(2,128)S(1)}, /*index=5*/s32[]{:T(128)}) while((s32[]{:T(128)}, bf16[2,1024,256]{2,1,0:T(8,128)(2,1)}, f32[2,2,1024]{2,1,0:T(2,128)S(1)}, ...), condition=%wide.region_3.4_spmd, body=%wide.region_0.3_spmd.sunk | while | flops 1100216320 | bytes 36778076 | solution.py:135
  98.3 4.6 convolution_convert_fusion.1
  102.9 6.9 %reshape.1037 = bf16[2,1024,3,2,128]{4,3,2,1,0:T(2,128)(2,1)} reshape(bf16[2048,768]{1,0:T(8,128)(2,1)} %convolution_convert_fusion.1) | data formatting | bytes 6291456 | tf_op jit(solution)/shard_map/reshape | solution.py:120
  109.8 4.1 copy.234
  114.9 20.6 %while.45 = (s32[]{:T(128)}, bf16[2,1024,256]{2,1,0:T(8,128)(2,1)}, f32[2,2,1024]{2,1,0:T(2,128)S(1)}, bf16[2,1024,3,2,128]{4,1,3,2,0:T(8,128)(2,1)}, s32[2,1024]{1,0:T(2,128)S(1)}, /*index=5*/s32[]{:T(128)}) while((s32[]{:T(128)}, bf16[2,1024,256]{2,1,0:T(8,128)(2,1)}, f32[2,2,1024]{2,1,0:T(2,128)S(1)}, ...), condition=%wide.region_7.8_spmd, body=%wide.region_4.7_spmd.sunk | while | flops 1100216320 | bytes 36778076 | solution.py:135
  143.6 5.2 multiply_convert_fusion.2
  159.0 4.2 reshape.1040
  314.2 31.5 %psum.14 = f32[]{:T(128)} all-reduce(f32[]{:T(128)S(6)} %add.330), channel_id=1, replica_groups=mesh['half'=2,'dp'=8,'mp'=2] {'dp','mp'}, use_global_device_ids=true, to_apply=%region_38.39 | all-reduce | flops 1 | bytes 8 | tf_op jit(solution)/shard_map/psum | solution.py:327
  361.7 4.3 copy.258
  382.2 5.3 fusion.55
  387.5 4.3 multiply_reduce_fusion.3
  419.0 35.3 %while.47 = (s32[]{:T(128)}, bf16[2,1024,768]{2,1,0:T(8,128)(2,1)}, bf16[2,1024,3,2,128]{4,1,3,2,0:T(8,128)(2,1)}, s32[2,1024]{1,0:T(2,128)S(1)}, f32[2,2,1024]{...) while((s32[]{:T(128)}, bf16[2,1024,768]{2,1,0:T(8,128)(2,1)}, ...), condition=%wide.region_54.55_spmd, body=%wide.region_52.54_spmd.sunk | while | flops 2719741952 | bytes 86052960 | solution.py:160
  458.4 35.5 %while.46 = (s32[]{:T(128)}, bf16[2,1024,768]{2,1,0:T(8,128)(2,1)}, bf16[2,1024,3,2,128]{4,1,3,2,0:T(8,128)(2,1)}, s32[2,1024]{1,0:T(2,128)S(1)}, f32[2,2,1024]{...) while((s32[]{:T(128)}, bf16[2,1024,768]{2,1,0:T(8,128)(2,1)}, ...), condition=%wide.region_51.52_spmd, body=%wide.region_49.51_spmd.sunk | while | flops 2719741952 | bytes 86052960 | solution.py:160
  493.9 4.1 fusion.263
  498.3 5.2 add_add_fusion
  534.9 5.1 collective-permute-done.31
  541.5 23.1 %collective-permute-done.33 = bf16[512,768]{1,0:T(8,128)(2,1)} collective-permute-done((bf16[512,768]{1,0:T(8,128)(2,1)}, bf16[512,768]{1,0:T(8,128)(2,1)}, u32[]{:S(2)}, u32[]{:S(2)}) %collective-permute-start.33) | collective-permute-done | bytes 786464 | tf_op jit(solution)/shard_map/ppermute | solution.py:31
  568.5 4.6 fusion.112
  573.2 14.8 %collective-permute-done.32 = f32[32,640]{1,0:T(8,128)S(1)} collective-permute-done((f32[32,640]{1,0:T(8,128)S(1)}, f32[32,640]{1,0:T(8,128)S(1)}, u32[]{:S(2)}, u32[]{:S(2)}) %collective-permute-start.32) | collective-permute-done | bytes 81952 | tf_op jit(solution)/shard_map/ppermute | solution.py:31
  602.9 4.5 collective-permute-done.40
  (734 shorter events, 442.4 us)
Async XLA Ops:
  7.2 510.6 %all-reduce.4.cloned.1.call-start = ((), (), s32[]{:S(2)}) async-start(), calls=%async_computation | async-start | bytes 1294336 | tf_op jit(solution)/shard_map/psum | solution.py:323
  8.0 17.3 %collective-permute-start = (bf16[32,768]{1,0:T(8,128)(2,1)S(1)}, bf16[32,768]{1,0:T(8,128)(2,1)S(1)}, u32[]{:S(2)}, u32[]{:S(2)}) collective-permute-start(bf16[32,768]{1,0:T(8,128)(2,1)S(1)} %bitcast.692), channel_id=1, source_target_pairs={{0,8},{2,10},{4,12},{6,14},{8,0},{10,2},{12,4},{14,6},{1,9},{3,11}... | collective-permute-start | bytes 147464 | tf_op jit(solution)/shard_map/ppermute | solution.py:31
  12.9 14.2 %collective-permute-start.5 = (bf16[32,1280]{1,0:T(8,128)(2,1)S(1)}, bf16[32,1280]{1,0:T(8,128)(2,1)S(1)}, u32[]{:S(2)}, u32[]{:S(2)}) collective-permute-start(bf16[32,1280]{1,0:T(8,128)(2,1)S(1)} %pad_maximum_fusion.26), channel_id=1, source_target_pairs={{0,1},{1,0},{2,3},{3,2},{4,5},{5,4},{6,7},{7,6},{8,9},{9,8},{10,11... | collective-permute-start | bytes 245768 | tf_op jit(solution)/shard_map/ppermute | solution.py:31
  27.9 8.1 %collective-permute-start.6 = (bf16[32,3200]{1,0:T(8,128)(2,1)S(1)}, bf16[32,3200]{1,0:T(8,128)(2,1)S(1)}, u32[]{:S(2)}, u32[]{:S(2)}) collective-permute-start(bf16[32,3200]{1,0:T(8,128)(2,1)S(1)} %constant_dynamic-update-slice_fusion.4), channel_id=1, source_target_pairs={{0,16},{16,0},{1,17},{17,1},{2,18},{18,2},{3,19},{19,3},{4,20},{20... | collective-permute-start | bytes 614408 | tf_op jit(solution)/shard_map/ppermute | solution.py:31
  30.1 8.7 %collective-permute-start.2 = (bf16[2,2,32,768]{3,2,0,1:T(8,128)(2,1)S(1)}, bf16[2,2,32,768]{3,2,0,1:T(8,128)(2,1)S(1)}, u32[]{:S(2)}, u32[]{:S(2)}) collective-permute-start(bf16[2,2,32,768]{3,2,0,1:T(8,128)(2,1)S(1)} %pad_maximum_fusion.24), channel_id=1, source_target_pairs={{0,16},{16,0},{1,17},{17,1},{2,18},{18,2},{3,19},{19,3},{4,20},{20... | collective-permute-start | bytes 589832 | tf_op jit(solution)/shard_map/ppermute | solution.py:31
  36.8 17.2 %collective-permute-start.7 = (bf16[2,32,3200]{2,1,0:T(8,128)(2,1)}, bf16[2,32,3200]{2,1,0:T(8,128)(2,1)S(1)}, u32[]{:S(2)}, u32[]{:S(2)}) collective-permute-start(bf16[2,32,3200]{2,1,0:T(8,128)(2,1)} %pad_maximum_fusion.20), channel_id=1, source_target_pairs={{0,8},{2,10},{4,12},{6,14},{8,0},{10,2},{12,4},{14,6},{1,9},{3,11}... | collective-permute-start | bytes 1228808 | tf_op jit(solution)/shard_map/ppermute | solution.py:31
  39.0 16.8 %collective-permute-start.3 = (bf16[2,2,2,32,768]{4,3,1,2,0:T(8,128)(2,1)S(1)}, bf16[2,2,2,32,768]{4,3,1,2,0:T(8,128)(2,1)S(1)}, u32[]{:S(2)}, u32[]{:S(2)}) collective-permute-start(bf16[2,2,2,32,768]{4,3,1,2,0:T(8,128)(2,1)S(1)} %pad_maximum_fusion.21), channel_id=1, source_target_pairs={{0,2},{2,0},{4,6},{6,4},{8,10},{10,8},{12,14},{14,12},{1,3},{3,1},... | collective-permute-start | bytes 1179656 | tf_op jit(solution)/shard_map/ppermute | solution.py:31
  55.8 38.7 %collective-permute-start.8 = (bf16[2,2,32,3200]{3,2,1,0:T(8,128)(2,1)}, bf16[2,2,32,3200]{3,2,1,0:T(8,128)(2,1)}, u32[]{:S(2)}, u32[]{:S(2)}) collective-permute-start(bf16[2,2,32,3200]{3,2,1,0:T(8,128)(2,1)} %pad_maximum_fusion.11), channel_id=1, source_target_pairs={{0,4},{2,6},{4,0},{6,2},{8,12},{10,14},{12,8},{14,10},{1,5},{3,7},... | collective-permute-start | bytes 2457608 | tf_op jit(solution)/shard_map/ppermute | solution.py:31
  56.9 41.3 %collective-permute-start.4 = (bf16[512,768]{1,0:T(8,128)(2,1)}, bf16[512,768]{1,0:T(8,128)(2,1)}, u32[]{:S(2)}, u32[]{:S(2)}) collective-permute-start(bf16[512,768]{1,0:T(8,128)(2,1)} %bitcast.54), channel_id=1, source_target_pairs={{0,1},{1,0},{2,3},{3,2},{4,5},{5,4},{6,7},{7,6},{8,9},{9,8},{10,11... | collective-permute-start | bytes 2359304 | tf_op jit(solution)/shard_map/ppermute | solution.py:31
  98.3 37.3 %collective-permute-start.9 = (bf16[2,2,2,32,3200]{4,3,2,1,0:T(8,128)(2,1)}, bf16[2,2,2,32,3200]{4,3,2,1,0:T(8,128)(2,1)}, u32[]{:S(2)}, u32[]{:S(2)}) collective-permute-start(bf16[2,2,2,32,3200]{4,3,2,1,0:T(8,128)(2,1)} %pad_maximum_fusion.5), channel_id=1, source_target_pairs={{0,2},{2,0},{4,6},{6,4},{8,10},{10,8},{12,14},{14,12},{1,3},{3,1},... | collective-permute-start | bytes 4915208 | tf_op jit(solution)/shard_map/ppermute | solution.py:31
  155.8 10.1 %collective-permute-start.11 = (f32[2,8,4]{1,2,0:T(4,128)S(1)}, f32[2,8,4]{1,2,0:T(4,128)S(1)}, u32[]{:S(2)}, u32[]{:S(2)}) collective-permute-start(f32[2,8,4]{1,2,0:T(4,128)S(1)} %select_reduce_fusion), channel_id=1, source_target_pairs={{0,2},{2,0},{4,6},{6,4},{8,10},{10,8},{12,14},{14,12},{1,3},{3,1},... | collective-permute-start | bytes 776 | tf_op jit(solution)/shard_map/ppermute | solution.py:31
  182.6 166.4 %collective-permute-start.43 = (bf16[16,512]{1,0:T(8,128)(2,1)}, bf16[16,512]{1,0:T(8,128)(2,1)}, u32[]{:S(2)}, u32[]{:S(2)}) collective-permute-start(bf16[16,512]{1,0:T(8,128)(2,1)} %convert_bitcast_fusion.1), channel_id=1, source_target_pairs={{0,1},{1,0},{16,17},{17,16},{2,3},{3,2},{18,19},{19,18},{4,5},{5,4... | collective-permute-start | bytes 49160 | tf_op jit(solution)/shard_map/ppermute | solution.py:298
  307.7 39.9 %collective-permute-start.23 = (f32[16,512]{1,0:T(8,128)S(1)}, f32[16,512]{1,0:T(8,128)S(1)}, u32[]{:S(2)}, u32[]{:S(2)}) collective-permute-start(f32[16,512]{1,0:T(8,128)S(1)} %get-tuple-element.411), channel_id=1, source_target_pairs={{0,17},{1,16},{16,1},{17,0},{2,19},{3,18},{18,3},{19,2},{4,21},{5,... | collective-permute-start | bytes 98312 | tf_op jit(solution)/shard_map/ppermute | solution.py:298
  308.6 38.9 %collective-permute-start.22 = (f32[16,512]{1,0:T(8,128)S(1)}, f32[16,512]{1,0:T(8,128)S(1)}, u32[]{:S(2)}, u32[]{:S(2)}) collective-permute-start(f32[16,512]{1,0:T(8,128)S(1)} %get-tuple-element.412), channel_id=1, source_target_pairs={{0,16},{1,17},{16,0},{17,1},{2,18},{3,19},{18,2},{19,3},{4,20},{5,... | collective-permute-start | bytes 98312 | tf_op jit(solution)/shard_map/ppermute | solution.py:298
  345.8 9.5 %collective-permute-start.21 = (f32[]{:T(128)}, f32[]{:T(128)}, u32[]{:S(2)}, u32[]{:S(2)}) collective-permute-start(f32[]{:T(128)} %psum.14), channel_id=1, source_target_pairs={{0,16},{16,0},{1,17},{17,1},{2,18},{18,2},{3,19},{19,3},{4,20},{20... | collective-permute-start | bytes 20 | tf_op jit(solution)/shard_map/ppermute | solution.py:31
  410.7 95.5 %collective-permute-start.28 = (bf16[2,2,2,32,640]{4,3,2,1,0:T(8,128)(2,1)}, bf16[2,2,2,32,640]{4,3,2,1,0:T(8,128)(2,1)}, u32[]{:S(2)}, u32[]{:S(2)}) collective-permute-start(bf16[2,2,2,32,640]{4,3,2,1,0:T(8,128)(2,1)} %fusion.120), channel_id=1, source_target_pairs={{0,2},{2,0},{4,6},{6,4},{8,10},{10,8},{12,14},{14,12},{1,3},{3,1},... | collective-permute-start | bytes 983048 | tf_op jit(solution)/shard_map/ppermute | solution.py:31
  509.0 19.8 %collective-permute-start.29 = (bf16[2,2,32,640]{3,2,1,0:T(8,128)(2,1)}, bf16[2,2,32,640]{3,2,1,0:T(8,128)(2,1)}, u32[]{:S(2)}, u32[]{:S(2)}) collective-permute-start(bf16[2,2,32,640]{3,2,1,0:T(8,128)(2,1)} %fusion.131), channel_id=1, source_target_pairs={{0,16},{16,0},{1,17},{17,1},{2,18},{18,2},{3,19},{19,3},{4,20},{20... | collective-permute-start | bytes 491528 | tf_op jit(solution)/shard_map/ppermute | solution.py:31
  515.7 76.0 %collective-permute-start.38 = (bf16[512,1280]{1,0:T(8,128)(2,1)}, bf16[512,1280]{1,0:T(8,128)(2,1)}, u32[]{:S(2)}, u32[]{:S(2)}) collective-permute-start(bf16[512,1280]{1,0:T(8,128)(2,1)} %pad_maximum_fusion.8), channel_id=1, source_target_pairs={{0,1},{1,0},{2,3},{3,2},{4,5},{5,4},{6,7},{7,6},{8,9},{9,8},{10,11... | collective-permute-start | bytes 3932168 | tf_op jit(solution)/shard_map/ppermute | solution.py:31
  516.4 48.1 %collective-permute-start.33 = (bf16[512,768]{1,0:T(8,128)(2,1)}, bf16[512,768]{1,0:T(8,128)(2,1)}, u32[]{:S(2)}, u32[]{:S(2)}) collective-permute-start(bf16[512,768]{1,0:T(8,128)(2,1)} %convolution_convert_fusion.4), channel_id=1, source_target_pairs={{0,1},{1,0},{2,3},{3,2},{4,5},{5,4},{6,7},{7,6},{8,9},{9,8},{10,11... | collective-permute-start | bytes 2359304 | tf_op jit(solution)/shard_map/ppermute | solution.py:31
  522.6 71.5 %collective-permute-start.27 = (bf16[2,1,512,512]{3,2,1,0:T(8,128)(2,1)}, bf16[2,1,512,512]{3,2,1,0:T(8,128)(2,1)}, u32[]{:S(2)}, u32[]{:S(2)}) collective-permute-start(bf16[2,1,512,512]{3,2,1,0:T(8,128)(2,1)} %fusion.86), channel_id=1, source_target_pairs={{0,1},{1,0},{2,3},{3,2},{4,5},{5,4},{6,7},{7,6},{8,9},{9,8},{10,11... | collective-permute-start | bytes 3145736 | tf_op jit(solution)/shard_map/ppermute | solution.py:31
  526.7 8.2 %collective-permute-start.44 = (bf16[32,4032]{1,0:T(8,128)(2,1)S(1)}, bf16[32,4032]{1,0:T(8,128)(2,1)S(1)}, u32[]{:S(2)}, u32[]{:S(2)}) collective-permute-start(bf16[32,4032]{1,0:T(8,128)(2,1)S(1)} %convert_element_type.441), channel_id=1, source_target_pairs={{0,16},{16,0},{1,17},{17,1},{2,18},{18,2},{3,19},{19,3},{4,20},{20... | collective-permute-start | bytes 774152 | tf_op jit(solution)/shard_map/ppermute | solution.py:31
  540.0 47.9 %collective-permute-start.32 = (f32[32,640]{1,0:T(8,128)S(1)}, f32[32,640]{1,0:T(8,128)S(1)}, u32[]{:S(2)}, u32[]{:S(2)}) collective-permute-start(f32[32,640]{1,0:T(8,128)S(1)} %bitcast_add_fusion.9), channel_id=1, source_target_pairs={{0,1},{1,0},{2,3},{3,2},{4,5},{5,4},{6,7},{7,6},{8,9},{9,8},{10,11... | collective-permute-start | bytes 245768 | tf_op jit(solution)/shard_map/ppermute | solution.py:31
  568.5 21.5 %collective-permute-start.34 = (bf16[2,2,2,32,768]{4,3,1,2,0:T(8,128)(2,1)}, bf16[2,2,2,32,768]{4,3,1,2,0:T(8,128)(2,1)}, u32[]{:S(2)}, u32[]{:S(2)}) collective-permute-start(bf16[2,2,2,32,768]{4,3,1,2,0:T(8,128)(2,1)} %fusion.119), channel_id=1, source_target_pairs={{0,2},{2,0},{4,6},{6,4},{8,10},{10,8},{12,14},{14,12},{1,3},{3,1},... | collective-permute-start | bytes 1179656 | tf_op jit(solution)/shard_map/ppermute | solution.py:31
  598.8 8.6 %collective-permute-start.40 = (bf16[2,2,32,1280]{3,2,0,1:T(8,128)(2,1)S(1)}, bf16[2,2,32,1280]{3,2,0,1:T(8,128)(2,1)S(1)}, u32[]{:S(2)}, u32[]{:S(2)}) collective-permute-start(bf16[2,2,32,1280]{3,2,0,1:T(8,128)(2,1)S(1)} %fusion.121), channel_id=1, source_target_pairs={{0,16},{16,0},{1,17},{17,1},{2,18},{18,2},{3,19},{19,3},{4,20},{20... | collective-permute-start | bytes 983048 | tf_op jit(solution)/shard_map/ppermute | solution.py:31
  (165 other events, 1699.8 us)
Sparse Core Ops, SparseCore 0:
  348.7 88.7 all-reduce.3
